TPU v7x, 256 devices: a whole 4x4x8 slice. The times are simulated.
256 devices in a mesh: seq: 64 (over z, x_hi, y), tp: 4 (over x_lo, core).
Axes of the slice: x: 4 (x_hi: 2, x_lo: 2; x = x_hi * 2 + x_lo), y: 4, z: 8, core: 2. Of those that a mesh axis runs over, the one named last changes fastest.
Arguments:
- hidden: bfloat16 [16384, 8192], P('seq', 'tp'), may hold values from -6 to 6
- kept_index: int32 [64, 128], P('seq'), may hold values from 0 to 255, as said below
- doc_ids: int32 [16384], P('seq'), may hold values from 0 to 127, never falling along the last dimension, each value on 1 to 512 neighbouring positions
- norm_gain: float32 [8192], replicated, may hold values from 0.5 to 1.5
- w_query: bfloat16 [8192, 4096], P('seq', 'tp'), as said below
- key_value_weight: bfloat16 [8192, 2, 1024], P('seq', None, 'tp'), as said below
Outputs:
- attended: bfloat16 [8192, 4096], P('seq', 'tp')
Inputs may be any that keep to these rules, and one draw needn't show every extreme that they name: `kept_index`: each row lists 128 distinct positions of its span in increasing order, always with the span's first and last token. `w_query`: a projection matrix. `key_value_weight`: a projection matrix.
All inputs are finite; a program needn't handle non-finite values.
Results may differ from a plain program's by a relative error of at most 0.0075.
Values may be sent and summed in bfloat16 or wider, within the bound.
A program may use at most 128 MiB of HBM per device.

v0:
```python
import jax
import jax.numpy as jnp
from jax import lax
from jax.sharding import PartitionSpec as P

HEAD_WIDTH = 128


norm_eps = 1e-05
rope_base = 10000.0


def partner(block, axis, apart):
    count = lax.axis_size(axis)
    route = []
    for low in range(count):
        high = low | 1 << apart
        if high != low and high < count:
            route += [(low, high), (high, low)]
    return lax.ppermute(block, axis, route)


def rms_normed(rows, gain):
    values = rows.astype(jnp.float32)
    mean_square = jnp.mean(values * values, axis=1, keepdims=True)
    return (values * lax.rsqrt(mean_square + norm_eps) * gain).astype(jnp.bfloat16)


def rotate(values, positions):
    half = values.shape[-1] // 2
    freqs = rope_base ** (-(jnp.arange(half, dtype=jnp.float32) * 2.0) / values.shape[-1])
    angles = positions.astype(jnp.float32)[:, None] * freqs[None, :]
    cosine = jnp.cos(angles)[:, None, :]
    sine = jnp.sin(angles)[:, None, :]
    first = values[..., :half]
    second = values[..., half:]
    return jnp.concatenate(
        [first * cosine - second * sine, second * cosine + first * sine], axis=-1
    )


def attend(query, keys, values, query_pos, query_doc, key_pos, key_doc):
    rows, q_heads, head_size = query.shape
    kv_heads = keys.shape[1]
    query_group = q_heads // kv_heads
    block = min(1024, rows)
    grouped = query.reshape(rows // block, block, kv_heads, query_group, head_size)
    pos_blocks = query_pos.reshape(rows // block, block)
    doc_blocks = query_doc.reshape(rows // block, block)

    def one_block(items):
        q_block, p_block, d_block = items
        scores = jnp.einsum(
            "qkgd,skd->kgqs", q_block, keys, preferred_element_type=jnp.float32
        ) * head_size ** (-0.5)
        allowed = (key_pos[None, :] <= p_block[:, None]) & (key_doc[None, :] == d_block[:, None])
        scores = jnp.where(allowed[None, None], scores, -1e30)
        top = jnp.max(scores, axis=-1, keepdims=True)
        expo = jnp.exp(scores - top)
        probs = (expo / jnp.sum(expo, axis=-1, keepdims=True)).astype(jnp.bfloat16)
        mixed = jnp.einsum("kgqs,skd->qkgd", probs, values, preferred_element_type=jnp.float32)
        return mixed.astype(jnp.bfloat16).reshape(block, q_heads * head_size)

    out = lax.map(one_block, (grouped, pos_blocks, doc_blocks))
    return out.reshape(rows, q_heads * head_size)


def pair_order(first, own, other):
    return jnp.where(
        first, jnp.concatenate([own, other], axis=0), jnp.concatenate([other, own], axis=0)
    )


def body(hidden, kept_index, doc_ids, norm_gain, w_query, key_value_weight):
    span = hidden.shape[0]
    kept_tokens = kept_index[0]
    count = kept_tokens.shape[0]
    side = lax.axis_index("seq") % 2
    first = side == 0
    columns = jnp.arange(span, dtype=jnp.int32)
    picks = kept_tokens[:, None] == columns[None, :]
    selected = jnp.dot(
        picks.astype(jnp.bfloat16), hidden, preferred_element_type=jnp.float32
    ).astype(jnp.bfloat16)
    own_doc = jnp.sum(jnp.where(picks, doc_ids[None, :], 0), axis=1)
    own_pos = kept_tokens + side * span
    q_cols = w_query.shape[1]
    kv_cols = key_value_weight.shape[2]
    features = lax.all_gather(selected, "tp", axis=1, tiled=True)
    normed_hidden = rms_normed(features, norm_gain)
    query = jnp.dot(
        normed_hidden,
        lax.all_gather(w_query, "seq", axis=0, tiled=True),
        preferred_element_type=jnp.float32,
    )
    key_value_rows = jnp.einsum(
        "rd,dkc->rkc",
        normed_hidden,
        lax.all_gather(key_value_weight, "seq", axis=0, tiled=True),
        preferred_element_type=jnp.float32,
    )
    rot_query = rotate(query.reshape(count, q_cols // HEAD_WIDTH, HEAD_WIDTH), own_pos).astype(
        jnp.bfloat16
    )
    rot_key = rotate(
        key_value_rows[:, 0].reshape(count, kv_cols // HEAD_WIDTH, HEAD_WIDTH), own_pos
    ).astype(jnp.bfloat16)
    value = (
        key_value_rows[:, 1].reshape(count, kv_cols // HEAD_WIDTH, HEAD_WIDTH).astype(jnp.bfloat16)
    )
    other_key, other_value, other_pos, other_doc = partner(
        (rot_key, value, own_pos, own_doc), "seq", 0
    )
    return attend(
        rot_query,
        pair_order(first, rot_key, other_key),
        pair_order(first, value, other_value),
        own_pos,
        own_doc,
        pair_order(first, own_pos, other_pos),
        pair_order(first, own_doc, other_doc),
    )


def solution(mesh):
    placed = (P("seq", "tp"), P("seq", None), P("seq"), P(), P("seq", "tp"), P("seq", None, "tp"))
    return jax.shard_map(
        body, mesh=mesh, in_specs=placed, out_specs=P("seq", "tp"), check_vma=False
    )
```

profile of v0, /device:TPU:8, one launch (start us, length us, event | category | flops | bytes accessed | tf_op | source)
XLA Modules:
  0.0 427.1 jit_solution(9687771708076642096)
XLA Ops:
  6.5 0.0 copy-start
  6.5 0.0 copy-start.5
  6.5 0.0 all-gather.4.cloned.1.call-start
  6.5 1.2 copy-done
  7.8 1.8 convolution_convert_fusion
  9.6 0.0 all-gather.4.cloned.1.call-update
  9.6 0.0 all-gather.6.cloned.1.call-start
  9.7 1.6 copy.20
  11.2 0.0 all-gather.6.cloned.1.call-update
  11.3 0.0 all-gather.8.cloned.1.call-start
  11.3 0.7 all-gather.8.cloned.1.call-update
  12.0 0.9 select_reduce_fusion
  12.9 2.3 collective-permute-start.2
  15.1 0.7 fusion.51
  15.8 0.0 collective-permute-start.1
  15.8 0.2 multiply_cosine_fusion
  16.0 0.7 add_bitcast_fusion
  16.7 0.7 copy.27
  17.4 0.7 copy.26
  18.1 0.0 collective-permute-done.2
  18.1 1.2 collective-permute-done.1
  19.3 0.8 compare_and_fusion
  20.1 24.0 %all-gather.4.cloned.1.call-done = bf16[128,8192]{1,0:T(8,128)(2,1)} async-done(((bf16[128,2048]{1,0:T(8,128)(2,1)}), bf16[128,8192]{1,0:T(8,128)(2,1)}) %all-gather.4.cloned.1.call-update) | async-done | bytes 2097168 | tf_op jit(solution)/shard_map/all_gather | solution.py:89
  44.1 2.1 fusion.1
  46.2 0.0 copy-start.1
  46.2 152.6 %all-gather.6.cloned.1.call-done = bf16[8192,2,256]{2,0,1:T(8,128)(2,1)} async-done(((bf16[128,2,256]{2,0,1:T(8,128)(2,1)}), bf16[8192,2,256]{2,0,1:T(8,128)(2,1)}) %all-gather.6.cloned.1.call-update) | async-done | bytes 8388624 | tf_op jit(solution)/shard_map/all_gather | solution.py:99
  198.8 0.0 copy-done.5
  198.8 5.3 %fusion.4 = f32[128,2,256]{2,0,1:T(8,128)S(1)} fusion(bf16[8192,2,256]{2,0,1:T(8,128)(2,1)} %all-gather.6.cloned.1.call-done, bf16[128,8192]{1,0:T(8,128)(2,1)} %all-gather.4.cloned.1.call-done, f32[8192]{0:T(1024)S(1)} %copy-done.5, f32[128]{0:T(128)S(1)} %add_rsqrt_fusion), kind=kOutput, calls=%fused_computation.7 | convolution fusion | flops 1077936128 | bytes 10781184 | tf_op jit(solution)/shard_map/rd,dkc->rkc/dot_general | solution.py:96
  204.2 0.1 copy.39
  204.3 0.6 collective-permute-start.3
  204.9 0.1 copy.38
  205.1 0.0 copy-start.2
  205.1 0.0 copy-start.3
  205.1 0.0 copy-start.4
  205.1 1.6 collective-permute-start
  206.7 201.7 %all-gather.8.cloned.1.call-done = bf16[8192,1024]{1,0:T(8,128)(2,1)} async-done(((bf16[128,1024]{1,0:T(8,128)(2,1)}), bf16[8192,1024]{1,0:T(8,128)(2,1)}) %all-gather.8.cloned.1.call-update) | async-done | bytes 16777232 | tf_op jit(solution)/shard_map/all_gather | solution.py:93
  408.4 0.0 copy-done.1
  408.4 8.2 %convolution_bitcast_fusion = f32[16,8,8,128]{3,1,2,0:T(8,128)S(1)} fusion(bf16[8192,1024]{1,0:T(8,128)(2,1)} %all-gather.8.cloned.1.call-done, bf16[128,8192]{1,0:T(8,128)(2,1)S(1)} %copy-done.1, f32[8192]{0:T(1024)} %param.9, f32[128]{0:T(128)S(1)} %add_rsqrt_fusion), kind=kOutput, calls=%fused_computation.14 | convolution fusion | flops 2151677952 | bytes 19431936 | tf_op jit(solution)/shard_map/dot_general | solution.py:91
  416.6 0.1 copy.40
  416.7 0.0 copy-done.2
  416.7 0.0 copy-done.3
  416.7 0.3 subtract_convert_fusion
  417.0 0.0 collective-permute-done.3
  417.1 0.0 copy-done.4
  417.1 1.5 fusion.52
  418.6 0.0 collective-permute-done
  418.6 1.2 convolution_convert_fusion.1
  419.8 0.9 copy.32
  (10 shorter events, 0.2 us)
Async XLA Ops:
  6.5 1.2 copy-start
  6.5 192.3 %copy-start.5 = (f32[8192]{0:T(1024)S(1)}, f32[8192]{0:T(1024)}, u32[]{:S(2)}) copy-start(f32[8192]{0:T(1024)} %param.9) | copy-start | bytes 98308
  6.5 37.6 %all-gather.4.cloned.1.call-start = ((), (), s32[]{:S(2)}) async-start(), calls=%async_computation | async-start | bytes 2621440 | tf_op jit(solution)/shard_map/all_gather | solution.py:89
  9.6 189.2 %all-gather.6.cloned.1.call-start = ((), (), s32[]{:S(2)}) async-start(), calls=%async_computation.1 | async-start | bytes 8519680 | tf_op jit(solution)/shard_map/all_gather | solution.py:99
  11.3 397.1 %all-gather.8.cloned.1.call-start = ((), (), s32[]{:S(2)}) async-start(), calls=%async_computation.2 | async-start | bytes 17039360 | tf_op jit(solution)/shard_map/all_gather | solution.py:93
  12.9 5.3 %collective-permute-start.2 = (s32[128]{0:T(128)S(1)}, s32[128]{0:T(128)S(1)}, u32[]{:S(2)}, u32[]{:S(2)}) collective-permute-start(s32[128]{0:T(128)S(1)} %select_reduce_fusion), channel_id=1, source_target_pairs={{0,4},{4,0},{8,12},{12,8},{16,20},{20,16},{24,28},{28,24},{32,36},... | collective-permute-start | bytes 1544 | tf_op jit(solution)/shard_map/ppermute | solution.py:20
  15.8 3.5 collective-permute-start.1
  46.2 362.2 %copy-start.1 = (bf16[128,8192]{1,0:T(8,128)(2,1)S(1)}, bf16[128,8192]{1,0:T(8,128)(2,1)}, u32[]{:S(2)}) copy-start(bf16[128,8192]{1,0:T(8,128)(2,1)} %all-gather.4.cloned.1.call-done) | copy-start | bytes 6291460
  204.3 212.7 %collective-permute-start.3 = (bf16[128,2,128]{0,2,1:T(8,128)(2,1)S(1)}, bf16[128,2,128]{0,2,1:T(8,128)(2,1)}, u32[]{:S(2)}, u32[]{:S(2)}) collective-permute-start(bf16[128,2,128]{0,2,1:T(8,128)(2,1)S(1)} %pad_maximum_fusion), channel_id=1, source_target_pairs={{0,4},{4,0},{8,12},{12,8},{16,20},{20,16},{24,28},{28,24},{32,36},... | collective-permute-start | bytes 196616 | tf_op jit(solution)/shard_map/ppermute | solution.py:20
  205.1 211.6 %copy-start.2 = (f32[128,64]{1,0:T(8,128)S(1)}, f32[128,64]{1,0:T(8,128)}, u32[]{:S(2)}) copy-start(f32[128,64]{1,0:T(8,128)} %copy.27) | copy-start | bytes 98308
  205.1 211.6 %copy-start.3 = (f32[128,64]{1,0:T(8,128)S(1)}, f32[128,64]{1,0:T(8,128)}, u32[]{:S(2)}) copy-start(f32[128,64]{1,0:T(8,128)} %copy.26) | copy-start | bytes 98308
  205.1 212.0 %copy-start.4 = (pred[128,256]{0,1:T(8,128)(4,1)S(1)}, pred[128,256]{0,1:T(8,128)(4,1)}, u32[]{:S(2)}) copy-start(pred[128,256]{0,1:T(8,128)(4,1)} %compare_and_fusion) | copy-start | bytes 98308
  205.1 213.5 %collective-permute-start = (bf16[128,2,128]{0,2,1:T(8,128)(2,1)S(1)}, bf16[128,2,128]{0,2,1:T(8,128)(2,1)}, u32[]{:S(2)}, u32[]{:S(2)}) collective-permute-start(bf16[128,2,128]{0,2,1:T(8,128)(2,1)S(1)} %bitcast.52), channel_id=1, source_target_pairs={{0,4},{4,0},{8,12},{12,8},{16,20},{20,16},{24,28},{28,24},{32,36},... | collective-permute-start | bytes 196616 | tf_op jit(solution)/shard_map/ppermute | solution.py:20
Sparse Core Ops, SparseCore 0:
  9.7 34.3 all-gather.3
  47.6 151.1 all-gather.5
  202.3 206.0 all-gather.7
where the time goes:
time: 428 us; the launch traced here: 427 us
  waiting for transfers between devices  380 us (89%)
  matrix products  18 us (4%)
  between operations  13.3 us (3%)
  other arithmetic  5.53 us (1%)
  local copies, waits for them, and re-layouts  5.49 us (1%)
  starting transfers between devices  4.59 us (1%)
    all_gather x1, waiting for transfers between devices, body(): lax.all_gather(w_query, 'seq', axis=0, tiled=True)  202 us
    all_gather x1, waiting for transfers between devices, body(): lax.all_gather(key_value_weight, 'seq', axis=0, tiled=True)  153 us
    all_gather x1, waiting for transfers between devices, body(): features = lax.all_gather(selected, 'tp', axis=1, tiled=True)  24 us
  transfers between devices with their start and end apart: 7, of which 4 were waited for; matrix products, arithmetic and copies ran while one was open for 6% of the time, Pallas kernels for 0%

commit v1 on v0

v1 whole, which is shorter than its diff:
```python
import functools
import math

import jax
import jax.numpy as jnp
from jax import lax
from jax.experimental import pallas as pl
from jax.experimental.pallas import tpu as pltpu
from jax.sharding import PartitionSpec as P

MESH = pl.DeviceIdType.MESH
HEAD = 128
KEPT = 128
SPAN = 256
WIDTH = 8192
QUARTER = 2048
CHUNK = 256
CHUNKS = 6
norm_eps = 1e-05
rope_base = 10000.0

GROUPS = ((0, 1, 2), (3, 4, 5))


def kernel(
    hidden, kept, docs, gain_all, wq, wkv, out,
    gain, asrc, abuf, wbuf, pbuf, rbuf, ssb, pdb, kvb, rots,
    gain_sem, w_send, w_recv, a_send, a_recv, f_send, f_recv, p_send, p_recv,
    s_send, s_recv, d_send, d_recv, k_send, k_recv,
):
    f32, bf16 = jnp.float32, jnp.bfloat16
    s = lax.axis_index("seq")
    t = lax.axis_index("tp")
    z, xh, y = s // 8, lax.rem(s // 4, 2), lax.rem(s, 4)
    xl, c = t // 2, lax.rem(t, 2)
    x = xh * 2 + xl
    place = xh * 4 + y
    side = lax.rem(s, 2)

    def at(zz, xx, yy, cc):
        return (zz * 8 + (xx // 2) * 4 + yy, lax.rem(xx, 2) * 2 + cc)

    def plane(dx, dy):
        return lax.rem(x + dx + 4, 4), lax.rem(y + dy + 4, 4)

    up = (lax.rem(s + 8, 64), t)
    down = (lax.rem(s + 56, 64), t)
    sibling = (s, xl * 2 + (1 - c))
    partner = (s + 1 - 2 * side, t)
    moves = [(dx, dy) for dx in range(4) for dy in range(4) if (dx, dy) != (0, 0)]

    gain_copy = pltpu.make_async_copy(gain_all.at[pl.ds(t * 16, 16)], gain, gain_sem)
    gain_copy.start()

    barrier = pltpu.get_barrier_semaphore()

    def greet(device):
        pl.semaphore_signal(barrier, inc=1, device_id=device, device_id_type=MESH)

    greet(up)
    greet(down)
    for dx, dy in moves:
        xx, yy = plane(dx, dy)
        greet(at(z, xx, yy, c))
    greet(sibling)
    greet((s, (1 - xl) * 2 + (1 - c)))

    wbuf[0, z] = wkv[:, 0:CHUNK]
    wbuf[1, z] = wkv[:, CHUNK : 2 * CHUNK]
    for n in range(2, CHUNKS):
        wbuf[n, z] = wq[:, (n - 2) * CHUNK : (n - 1) * CHUNK]

    lane = lax.broadcasted_iota(jnp.int32, (KEPT, KEPT), 1)
    eye = lax.broadcasted_iota(jnp.int32, (KEPT, KEPT), 0) == lane

    def to_column(row):
        return jnp.sum(jnp.where(eye, jnp.broadcast_to(row, (KEPT, KEPT)), 0.0), axis=1, keepdims=True)

    def to_row(column):
        return jnp.sum(jnp.where(eye, jnp.broadcast_to(column, (KEPT, KEPT)), 0.0), axis=0, keepdims=True)

    kept_row = kept[...].astype(f32)
    kept_col = to_column(kept_row)
    columns = lax.broadcasted_iota(jnp.int32, (KEPT, SPAN), 1).astype(f32)
    picks = columns == kept_col
    chosen = jnp.where(picks, 1.0, 0.0).astype(bf16)
    doc_col = jnp.sum(jnp.where(picks, docs[...].astype(f32), 0.0), axis=1, keepdims=True)
    pos_row = kept_row + (side * SPAN).astype(f32)
    pos_col = kept_col + (side * SPAN).astype(f32)
    pdb[side, 0:1, :] = pos_row
    pdb[side, 1:2, :] = to_row(doc_col)

    gain_copy.wait()
    square = jnp.zeros((KEPT, 1), f32)
    for j in range(QUARTER // 256):
        rows = jnp.dot(chosen, hidden[:, j * 256 : (j + 1) * 256], preferred_element_type=f32)
        square += jnp.sum(rows * rows, axis=1, keepdims=True)
        for b in range(2):
            block = 2 * j + b
            scaled = rows[:, b * 128 : (b + 1) * 128] * gain[block : block + 1, :]
            high, to = block // 8, block % 8
            asrc[to, :, high * 128 : (high + 1) * 128] = scaled.astype(bf16)
    ssb[t, 0:1, :] = to_row(square)
    abuf[t, place] = asrc[place]

    pl.semaphore_wait(barrier, 19)

    def remote(src, dst, send, recv, device):
        return pltpu.make_async_remote_copy(
            src_ref=src, dst_ref=dst, send_sem=send, recv_sem=recv, device_id=device, device_id_type=MESH
        )

    sent = []

    def hops(n, way):
        return 4 if (n + way) % 2 == 0 else 3

    def w_copy(n, way, hop):
        origin = lax.rem(z + 8 - (hop - 1), 8) if way == 0 else lax.rem(z + hop - 1, 8)
        slot = wbuf.at[n, origin]
        return remote(slot, slot, w_send.at[n, way, hop - 1], w_recv.at[n, way, hop - 1], up if way == 0 else down)

    def w_arrived(n, way, hop):
        origin = lax.rem(z + 8 - hop, 8) if way == 0 else lax.rem(z + hop, 8)
        slot = wbuf.at[n, origin]
        remote(slot, slot, w_send.at[n, way, hop - 1], w_recv.at[n, way, hop - 1], up if way == 0 else down).wait_recv()

    def w_start(n, hop):
        for way in range(2):
            if hop <= hops(n, way):
                copy = w_copy(n, way, hop)
                copy.start()
                sent.append(copy)

    def w_wait(n, hop):
        for way in range(2):
            if hop <= hops(n, way):
                w_arrived(n, way, hop)

    def w_pass(n, hop):
        for way in range(2):
            if hop <= hops(n, way):
                w_arrived(n, way, hop)
                if hop + 1 <= hops(n, way):
                    copy = w_copy(n, way, hop + 1)
                    copy.start()
                    sent.append(copy)

    for n in GROUPS[0]:
        w_start(n, 1)

    a_copies = []
    for k, (dx, dy) in enumerate(moves):
        xx, yy = plane(dx, dy)
        copy = remote(asrc.at[(xx // 2) * 4 + yy], abuf.at[t, place], a_send.at[k], a_recv.at[k], at(z, xx, yy, c))
        copy.start()
        sent.append(copy)
    for k in range(1, 4):
        copy = remote(ssb.at[t], ssb.at[t], s_send.at[k - 1], s_recv.at[k - 1], (s, lax.rem(t + k, 4)))
        copy.start()
        sent.append(copy)
    copy = remote(pdb.at[side], pdb.at[side], d_send, d_recv, partner)
    copy.start()
    sent.append(copy)

    freqs = jnp.exp(lax.rem(lane, 64).astype(f32) * (-2.0 * math.log(rope_base) / HEAD))
    angles = pos_col * freqs
    rots[0] = jnp.cos(angles)
    sine = jnp.sin(angles)
    rots[1] = jnp.where(lane < 64, -sine, sine)

    for hop in range(1, 4):
        for n in GROUPS[0]:
            w_pass(n, hop)

    f_copies = []
    for dx in range(4):
        for dy in range(4):
            if (dx, dy) == (0, 0):
                continue
            k = moves.index((dx, dy))
            xx, yy = plane(-dx, -dy)
            slot = abuf.at[lax.rem(xx, 2) * 2 + c, (xx // 2) * 4 + yy]
            remote(slot, slot, a_send.at[k], a_recv.at[k], at(z, xx, yy, c)).wait_recv()
        xx, _ = plane(-dx, 0)
        block = abuf.at[lax.rem(xx, 2) * 2 + c, pl.ds((xx // 2) * 4, 4)]
        copy = remote(block, block, f_send.at[dx], f_recv.at[dx], sibling)
        copy.start()
        sent.append(copy)
    for n in GROUPS[1]:
        w_start(n, 1)
    for dx in range(4):
        xx, _ = plane(-dx, 0)
        block = abuf.at[lax.rem(xx, 2) * 2 + (1 - c), pl.ds((xx // 2) * 4, 4)]
        remote(block, block, f_send.at[dx], f_recv.at[dx], sibling).wait_recv()

    def product(n):
        def half(r):
            total = jnp.zeros((512, CHUNK), f32)
            for q in range(4):
                total += jnp.dot(
                    abuf[q, pl.ds(r * 4, 4)].reshape(512, 256),
                    wbuf[n, 2 * q : 2 * q + 2].reshape(256, CHUNK),
                    preferred_element_type=f32,
                )
            pbuf[n, pl.ds(r * 4, 4)] = total.astype(bf16).reshape(4, KEPT, CHUNK)

        pl.loop(0, 2)(half)
        for k in range(1, 8):
            xx, yy = lax.rem(x + 2 * (k // 4), 4), lax.rem(y + k % 4, 4)
            copy = remote(
                pbuf.at[n, (xx // 2) * 4 + yy], rbuf.at[n, k - 1], p_send.at[n, k - 1], p_recv.at[n, k - 1],
                at(z, xx, yy, c),
            )
            copy.start()
            sent.append(copy)

    def summed(n):
        total = pbuf[n, place].astype(f32)
        for k in range(1, 8):
            slot = rbuf.at[n, k - 1]
            remote(slot, slot, p_send.at[n, k - 1], p_recv.at[n, k - 1], sibling).wait_recv()
            total += rbuf[n, k - 1].astype(f32)
        return total * scale

    def rotated(block):
        heads = []
        for h in range(2):
            head = block[:, h * HEAD : (h + 1) * HEAD]
            heads.append((head * rots[0] + pltpu.roll(head, 64, 1) * rots[1]).astype(bf16))
        return heads

    for n in GROUPS[0]:
        w_wait(n, 4)
        product(n)

    for k in range(1, 4):
        slot = ssb.at[lax.rem(t + 4 - k, 4)]
        remote(slot, slot, s_send.at[k - 1], s_recv.at[k - 1], sibling).wait_recv()
    squares = ssb[0, 0:1, :] + ssb[1, 0:1, :] + ssb[2, 0:1, :] + ssb[3, 0:1, :]
    scale = lax.rsqrt(to_column(squares) * (1.0 / WIDTH) + norm_eps)

    slot = pdb.at[1 - side]
    remote(slot, slot, d_send, d_recv, partner).wait_recv()
    key_pos = jnp.concatenate([pdb[0, 0:1, :], pdb[1, 0:1, :]], axis=1)
    key_doc = jnp.concatenate([pdb[0, 1:2, :], pdb[1, 1:2, :]], axis=1)
    allowed = (key_pos <= pos_col) & (key_doc == doc_col)

    def share(j):
        rows = kvb.at[j, side]
        copy = remote(rows, rows, k_send.at[j], k_recv.at[j], partner)
        copy.start()
        sent.append(copy)

    def keys():
        first, second = rotated(summed(0))
        kvb[0, side, :, 0:HEAD] = first
        kvb[0, side, :, HEAD : 2 * HEAD] = second
        share(0)

    def values():
        kvb[1, side] = summed(1).astype(bf16)
        share(1)

    def attend(n):
        head = (n - 2) // 2
        queries = rotated(summed(n))
        key = kvb[0, :, :, head * HEAD : (head + 1) * HEAD].reshape(2 * KEPT, HEAD)
        value = kvb[1, :, :, head * HEAD : (head + 1) * HEAD].reshape(2 * KEPT, HEAD)
        for h in range(2):
            score = lax.dot_general(
                queries[h], key, (((1,), (1,)), ((), ())), preferred_element_type=f32
            ) * (HEAD ** -0.5)
            score = jnp.where(allowed, score, -1e30)
            top = jnp.max(score, axis=1, keepdims=True)
            expo = jnp.exp(score - top)
            norm = jnp.sum(expo, axis=1, keepdims=True)
            mixed = jnp.dot(expo.astype(bf16), value, preferred_element_type=f32) / norm
            place_at = ((n - 2) * 2 + h) * HEAD
            out[:, place_at : place_at + HEAD] = mixed.astype(bf16)

    for n in GROUPS[1]:
        w_pass(n, 1)
    keys()
    for n in GROUPS[1]:
        w_pass(n, 2)
    values()
    for n in GROUPS[1]:
        w_pass(n, 3)
    for n in GROUPS[1]:
        w_wait(n, 4)
        product(n)
    for j in range(2):
        slot = kvb.at[j, 1 - side]
        remote(slot, slot, k_send.at[j], k_recv.at[j], partner).wait_recv()
    for n in range(2, CHUNKS):
        attend(n)
    for copy in sent:
        copy.wait_send()


def body(hidden, kept_index, doc_ids, norm_gain, w_query, key_value_weight):
    f32, bf16 = jnp.float32, jnp.bfloat16
    dma = pltpu.SemaphoreType.DMA
    vmem = pl.BlockSpec(memory_space=pltpu.VMEM)
    return pl.pallas_call(
        kernel,
        out_shape=jax.ShapeDtypeStruct((KEPT, 1024), bf16),
        in_specs=[vmem, vmem, vmem, pl.BlockSpec(memory_space=pl.ANY), vmem, vmem],
        out_specs=vmem,
        scratch_shapes=[
            pltpu.VMEM((16, 128), f32),
            pltpu.VMEM((8, KEPT, 256), bf16),
            pltpu.VMEM((4, 8, KEPT, 256), bf16),
            pltpu.VMEM((CHUNKS, 8, 128, CHUNK), bf16),
            pltpu.VMEM((CHUNKS, 8, KEPT, CHUNK), bf16),
            pltpu.VMEM((CHUNKS, 7, KEPT, CHUNK), bf16),
            pltpu.VMEM((4, 8, 128), f32),
            pltpu.VMEM((2, 8, 128), f32),
            pltpu.VMEM((2, 2, KEPT, 256), bf16),
            pltpu.VMEM((2, KEPT, HEAD), f32),
            dma,
            dma((CHUNKS, 2, 4)), dma((CHUNKS, 2, 4)),
            dma((15,)), dma((15,)),
            dma((4,)), dma((4,)),
            dma((CHUNKS, 7)), dma((CHUNKS, 7)),
            dma((3,)), dma((3,)),
            dma, dma,
            dma((2,)), dma((2,)),
        ],
        compiler_params=pltpu.CompilerParams(
            collective_id=0, has_side_effects=True, vmem_limit_bytes=48 * 1024 * 1024
        ),
    )(
        hidden, kept_index, doc_ids.reshape(1, SPAN), norm_gain.reshape(WIDTH // 128, 128),
        w_query, key_value_weight.reshape(128, 512),
    )


def solution(mesh):
    placed = (P("seq", "tp"), P("seq", None), P("seq"), P(), P("seq", "tp"), P("seq", None, "tp"))
    return jax.shard_map(
        body, mesh=mesh, in_specs=placed, out_specs=P("seq", "tp"), check_vma=False
    )
```

time: 428 us -> 75.9 us (0.18)
  the two profiles are of different devices: /device:TPU:8 before, /device:TPU:1 now
where the time goes in v1:
time: 75.9 us; the launch traced here: 75.7 us
  Pallas kernels  71.3 us (94%)
  local copies, waits for them, and re-layouts  4.33 us (6%)
    pallas_call x1, Pallas kernels, body(): pl.pallas_call(kernel, out_shape=jax.ShapeDtypeStruct((KEPT, 1024), bf16)...  71.3 us
    unnamed x12, local copies, waits for them, and re-layouts  4.33 us

profile of v1, /device:TPU:1, one launch (start us, length us, event | category | flops | bytes accessed | tf_op | source)
XLA Modules:
  0.0 75.7 jit_solution(1270648880432280555)
XLA Ops:
  0.0 0.0 copy-start.1
  0.0 1.0 %copy.7 = bf16[16,8,2,256]{3,1,2,0:T(8,128)(2,1)S(1)} copy(bf16[16,8,2,256]{3,2,1,0:T(2,128)(2,1)} %bitcast.7) | data formatting | bytes 262144
  1.0 0.0 copy-start.3
  1.0 0.0 copy-start.4
  1.0 0.0 copy-done.1
  1.0 0.6 copy-done.3
  1.7 0.0 copy-done.4
  1.7 0.0 copy-start
  1.7 1.2 %copy-done = bf16[256,2048]{1,0:T(8,128)(2,1)S(1)} copy-done((bf16[256,2048]{1,0:T(8,128)(2,1)S(1)}, bf16[256,2048]{1,0:T(8,128)(2,1)}, u32[]{:S(2)}) %copy-start) | copy-done | bytes 1048600
  2.9 0.0 copy-start.2
  2.9 0.8 copy-done.2
  3.6 71.3 %shard_map.64 = bf16[128,1024]{1,0:T(8,128)(2,1)S(1)} custom-call(bf16[256,2048]{1,0:T(8,128)(2,1)S(1)} %copy-done, s32[1,128]{1,0:T(1,128)S(1)} %copy-done.4, s32[1,256]{1,0:T(1,128)S(1)} %bitcast.6, f32[64,128]{1,0:T(8,128)S(1)} %bitcast.5, bf16[128,1024]{1,0:T(8,128)(2,1)S(1)} %copy-done.1, bf16[128,512]{1,0:T(8,128)(2,1)S(1)} %bitcast.4), custom_call_target="tpu_custom_call" | custom-call | tf_op jit(solution)/shard_map/pallas_call | solution.py:306
  75.0 0.7 copy.9
Async XLA Ops:
  0.0 1.0 %copy-start.1 = (bf16[128,1024]{1,0:T(8,128)(2,1)S(1)}, bf16[128,1024]{1,0:T(8,128)(2,1)}, u32[]{:S(2)}) copy-start(bf16[128,1024]{1,0:T(8,128)(2,1)} %wq.1) | copy-start | bytes 786436
  1.0 0.7 copy-start.3
  1.0 0.7 copy-start.4
  1.7 1.2 %copy-start = (bf16[256,2048]{1,0:T(8,128)(2,1)S(1)}, bf16[256,2048]{1,0:T(8,128)(2,1)}, u32[]{:S(2)}) copy-start(bf16[256,2048]{1,0:T(8,128)(2,1)} %hidden.1) | copy-start | bytes 3145732
  2.9 0.8 %copy-start.2 = (f32[8192]{0:T(1024)S(1)}, f32[8192]{0:T(1024)}, u32[]{:S(2)}) copy-start(f32[8192]{0:T(1024)} %param.9) | copy-start | bytes 98308

commit v2 on v1

--- a/solution.py
+++ b/solution.py
@@ -20,12 +20,13 @@
 rope_base = 10000.0
 
 GROUPS = ((0, 1, 2), (3, 4, 5))
+X_FIRST = (True, False, True, False, True, False)
 
 
 def kernel(
-    hidden, kept, docs, gain_all, wq, wkv, out,
-    gain, asrc, abuf, wbuf, pbuf, rbuf, ssb, pdb, kvb, rots,
-    gain_sem, w_send, w_recv, a_send, a_recv, f_send, f_recv, p_send, p_recv,
+    hidden_in, kept_in, docs_in, gain_in, wq, wkv_in, out,
+    hidden, kept, docs, gain, wkv, asrc, abuf, wbuf, pbuf, qbuf, rbuf, ssb, pdb, kvb, rots,
+    load_sem, w_send, w_recv, a_send, a_recv, f_send, f_recv, p_send, p_recv,
     s_send, s_recv, d_send, d_recv, k_send, k_recv,
 ):
     f32, bf16 = jnp.float32, jnp.bfloat16
@@ -49,9 +50,6 @@
     partner = (s + 1 - 2 * side, t)
     moves = [(dx, dy) for dx in range(4) for dy in range(4) if (dx, dy) != (0, 0)]
 
-    gain_copy = pltpu.make_async_copy(gain_all.at[pl.ds(t * 16, 16)], gain, gain_sem)
-    gain_copy.start()
-
     barrier = pltpu.get_barrier_semaphore()
 
     def greet(device):
@@ -65,10 +63,21 @@
     greet(sibling)
     greet((s, (1 - xl) * 2 + (1 - c)))
 
-    wbuf[0, z] = wkv[:, 0:CHUNK]
-    wbuf[1, z] = wkv[:, CHUNK : 2 * CHUNK]
-    for n in range(2, CHUNKS):
-        wbuf[n, z] = wq[:, (n - 2) * CHUNK : (n - 1) * CHUNK]
+    loads = [
+        pltpu.make_async_copy(src, dst, load_sem.at[i])
+        for i, (src, dst) in enumerate(
+            [
+                (kept_in, kept),
+                (docs_in, docs),
+                (hidden_in, hidden),
+                (gain_in.at[pl.ds(t * 16, 16)], gain),
+                (wkv_in, wkv),
+            ]
+            + [(wq.at[:, pl.ds(n * CHUNK, CHUNK)], wbuf.at[n + 2, z]) for n in range(4)]
+        )
+    ]
+    for load in loads:
+        load.start()
 
     lane = lax.broadcasted_iota(jnp.int32, (KEPT, KEPT), 1)
     eye = lax.broadcasted_iota(jnp.int32, (KEPT, KEPT), 0) == lane
@@ -79,6 +88,8 @@
     def to_row(column):
         return jnp.sum(jnp.where(eye, jnp.broadcast_to(column, (KEPT, KEPT)), 0.0), axis=0, keepdims=True)
 
+    loads[0].wait()
+    loads[1].wait()
     kept_row = kept[...].astype(f32)
     kept_col = to_column(kept_row)
     columns = lax.broadcasted_iota(jnp.int32, (KEPT, SPAN), 1).astype(f32)
@@ -90,7 +101,8 @@
     pdb[side, 0:1, :] = pos_row
     pdb[side, 1:2, :] = to_row(doc_col)
 
-    gain_copy.wait()
+    loads[2].wait()
+    loads[3].wait()
     square = jnp.zeros((KEPT, 1), f32)
     for j in range(QUARTER // 256):
         rows = jnp.dot(chosen, hidden[:, j * 256 : (j + 1) * 256], preferred_element_type=f32)
@@ -102,6 +114,10 @@
             asrc[to, :, high * 128 : (high + 1) * 128] = scaled.astype(bf16)
     ssb[t, 0:1, :] = to_row(square)
     abuf[t, place] = asrc[place]
+    for load in loads[4:]:
+        load.wait()
+    wbuf[0, z] = wkv[:, 0, :]
+    wbuf[1, z] = wkv[:, 1, :]
 
     pl.semaphore_wait(barrier, 19)
 
@@ -149,7 +165,6 @@
     for n in GROUPS[0]:
         w_start(n, 1)
 
-    a_copies = []
     for k, (dx, dy) in enumerate(moves):
         xx, yy = plane(dx, dy)
         copy = remote(asrc.at[(xx // 2) * 4 + yy], abuf.at[t, place], a_send.at[k], a_recv.at[k], at(z, xx, yy, c))
@@ -173,7 +188,6 @@
         for n in GROUPS[0]:
             w_pass(n, hop)
 
-    f_copies = []
     for dx in range(4):
         for dy in range(4):
             if (dx, dy) == (0, 0):
@@ -206,21 +220,55 @@
             pbuf[n, pl.ds(r * 4, 4)] = total.astype(bf16).reshape(4, KEPT, CHUNK)
 
         pl.loop(0, 2)(half)
-        for k in range(1, 8):
-            xx, yy = lax.rem(x + 2 * (k // 4), 4), lax.rem(y + k % 4, 4)
-            copy = remote(
-                pbuf.at[n, (xx // 2) * 4 + yy], rbuf.at[n, k - 1], p_send.at[n, k - 1], p_recv.at[n, k - 1],
-                at(z, xx, yy, c),
-            )
+        for slot, block, device in first_step(n):
+            copy = remote(pbuf.at[n, block], rbuf.at[n, slot], p_send.at[n, slot], p_recv.at[n, slot], device)
             copy.start()
             sent.append(copy)
 
+    across = at(z, lax.rem(x + 2, 4), y, c)
+    far_place = (1 - xh) * 4 + y
+
+    def along(dy):
+        return lax.rem(y + dy, 4)
+
+    def first_step(n):
+        if X_FIRST[n]:
+            return [(dy, (1 - xh) * 4 + along(dy), across) for dy in (2, 1, 3, 0)]
+        return [
+            (3 * own + dy - 1, (xh if own else 1 - xh) * 4 + along(dy), at(z, x, along(dy), c))
+            for own in range(2)
+            for dy in (2, 1, 3)
+        ]
+
+    def arrived(n, slot):
+        ref = rbuf.at[n, slot]
+        remote(ref, ref, p_send.at[n, slot], p_recv.at[n, slot], across).wait_recv()
+        return rbuf[n, slot].astype(f32)
+
+    def second_step(n):
+        if X_FIRST[n]:
+            for dy in (2, 1, 3):
+                total = pbuf[n, xh * 4 + along(dy)].astype(f32) + arrived(n, dy)
+                qbuf[n, dy - 1] = total.astype(bf16)
+                copy = remote(
+                    qbuf.at[n, dy - 1], rbuf.at[n, 3 + dy], p_send.at[n, 3 + dy], p_recv.at[n, 3 + dy],
+                    at(z, x, along(dy), c),
+                )
+                copy.start()
+                sent.append(copy)
+        else:
+            total = pbuf[n, far_place].astype(f32)
+            for dy in (1, 3, 2):
+                total += arrived(n, dy - 1)
+            qbuf[n, 0] = total.astype(bf16)
+            copy = remote(qbuf.at[n, 0], rbuf.at[n, 6], p_send.at[n, 6], p_recv.at[n, 6], across)
+            copy.start()
+            sent.append(copy)
+
     def summed(n):
         total = pbuf[n, place].astype(f32)
-        for k in range(1, 8):
-            slot = rbuf.at[n, k - 1]
-            remote(slot, slot, p_send.at[n, k - 1], p_recv.at[n, k - 1], sibling).wait_recv()
-            total += rbuf[n, k - 1].astype(f32)
+        for slot in (0, 4, 6, 5) if X_FIRST[n] else (3, 5, 4, 6):
+            total += arrived(n, slot)
         return total * scale
 
     def rotated(block):
@@ -279,22 +327,33 @@
             place_at = ((n - 2) * 2 + h) * HEAD
             out[:, place_at : place_at + HEAD] = mixed.astype(bf16)
 
+    def joined():
+        for j in range(2):
+            slot = kvb.at[j, 1 - side]
+            remote(slot, slot, k_send.at[j], k_recv.at[j], partner).wait_recv()
+
     for n in GROUPS[1]:
         w_pass(n, 1)
-    keys()
     for n in GROUPS[1]:
         w_pass(n, 2)
-    values()
+    second_step(0)
+    second_step(1)
     for n in GROUPS[1]:
         w_pass(n, 3)
+    values()
+    keys()
     for n in GROUPS[1]:
         w_wait(n, 4)
         product(n)
-    for j in range(2):
-        slot = kvb.at[j, 1 - side]
-        remote(slot, slot, k_send.at[j], k_recv.at[j], partner).wait_recv()
-    for n in range(2, CHUNKS):
-        attend(n)
+    second_step(2)
+    joined()
+    attend(2)
+    second_step(3)
+    second_step(4)
+    attend(3)
+    second_step(5)
+    attend(4)
+    attend(5)
     for copy in sent:
         copy.wait_send()
 
@@ -306,20 +365,25 @@
     return pl.pallas_call(
         kernel,
         out_shape=jax.ShapeDtypeStruct((KEPT, 1024), bf16),
-        in_specs=[vmem, vmem, vmem, pl.BlockSpec(memory_space=pl.ANY), vmem, vmem],
+        in_specs=[pl.BlockSpec(memory_space=pl.ANY)] * 6,
         out_specs=vmem,
         scratch_shapes=[
+            pltpu.VMEM((SPAN, QUARTER), bf16),
+            pltpu.VMEM((1, KEPT), jnp.int32),
+            pltpu.VMEM((1, SPAN), jnp.int32),
             pltpu.VMEM((16, 128), f32),
+            pltpu.VMEM((128, 2, 256), bf16),
             pltpu.VMEM((8, KEPT, 256), bf16),
             pltpu.VMEM((4, 8, KEPT, 256), bf16),
             pltpu.VMEM((CHUNKS, 8, 128, CHUNK), bf16),
             pltpu.VMEM((CHUNKS, 8, KEPT, CHUNK), bf16),
+            pltpu.VMEM((CHUNKS, 3, KEPT, CHUNK), bf16),
             pltpu.VMEM((CHUNKS, 7, KEPT, CHUNK), bf16),
             pltpu.VMEM((4, 8, 128), f32),
             pltpu.VMEM((2, 8, 128), f32),
             pltpu.VMEM((2, 2, KEPT, 256), bf16),
             pltpu.VMEM((2, KEPT, HEAD), f32),
-            dma,
+            dma((9,)),
             dma((CHUNKS, 2, 4)), dma((CHUNKS, 2, 4)),
             dma((15,)), dma((15,)),
             dma((4,)), dma((4,)),
@@ -329,11 +393,11 @@
             dma((2,)), dma((2,)),
         ],
         compiler_params=pltpu.CompilerParams(
-            collective_id=0, has_side_effects=True, vmem_limit_bytes=48 * 1024 * 1024
+            collective_id=0, has_side_effects=True, vmem_limit_bytes=56 * 1024 * 1024
         ),
     )(
         hidden, kept_index, doc_ids.reshape(1, SPAN), norm_gain.reshape(WIDTH // 128, 128),
-        w_query, key_value_weight.reshape(128, 512),
+        w_query, key_value_weight,
     )
 
 

time: 75.9 us -> 75.7 us (level)
  the two profiles are of different devices: /device:TPU:1 before, /device:TPU:8 now
where the time goes in v2:
time: 75.7 us; the launch traced here: 75.6 us
  Pallas kernels  73.9 us (98%)
  local copies, waits for them, and re-layouts  1.67 us (2%)
    pallas_call x1, Pallas kernels, body(): pl.pallas_call(kernel, out_shape=jax.ShapeDtypeStruct((KEPT, 1024), bf16)...  73.9 us
    unnamed x1, local copies, waits for them, and re-layouts  1.67 us

profile of v2, /device:TPU:8, one launch (start us, length us, event | category | flops | bytes accessed | tf_op | source)
XLA Modules:
  0.0 75.6 jit_solution(11240261370824994386)
XLA Ops:
  0.0 73.9 %shard_map.64 = bf16[128,1024]{1,0:T(8,128)(2,1)} custom-call(bf16[256,2048]{1,0:T(8,128)(2,1)} %hidden_in.1, s32[1,128]{1,0:T(1,128)} %kept_in.1, s32[1,256]{1,0:T(1,128)} %bitcast.3, f32[64,128]{1,0:T(8,128)} %bitcast.2, bf16[128,1024]{1,0:T(8,128)(2,1)} %wq.1, bf16[128,2,256]{2,1,0:T(2,128)(2,1)} %wkv_in.1), custom_call_target="tpu_custom_call" | custom-call | tf_op jit(solution)/shard_map/pallas_call | solution.py:365
  73.9 1.7 %copy.8 = bf16[128,1024]{1,0:T(8,128)(2,1)} copy(bf16[128,1024]{1,0:T(8,128)(2,1)} %shard_map.64) | data formatting | bytes 524288

commit v3 on v2

--- a/solution.py
+++ b/solution.py
@@ -19,8 +19,7 @@
 norm_eps = 1e-05
 rope_base = 10000.0
 
-GROUPS = ((0, 1, 2), (3, 4, 5))
-X_FIRST = (True, False, True, False, True, False)
+X_FIRST = (False, True, False, True, False, True)
 
 
 def kernel(
@@ -49,6 +48,7 @@
     sibling = (s, xl * 2 + (1 - c))
     partner = (s + 1 - 2 * side, t)
     moves = [(dx, dy) for dx in range(4) for dy in range(4) if (dx, dy) != (0, 0)]
+    moves.sort(key=lambda m: -min(m[0], 4 - m[0]) - min(m[1], 4 - m[1]))
 
     barrier = pltpu.get_barrier_semaphore()
 
@@ -131,39 +131,30 @@
     def hops(n, way):
         return 4 if (n + way) % 2 == 0 else 3
 
-    def w_copy(n, way, hop):
-        origin = lax.rem(z + 8 - (hop - 1), 8) if way == 0 else lax.rem(z + hop - 1, 8)
-        slot = wbuf.at[n, origin]
-        return remote(slot, slot, w_send.at[n, way, hop - 1], w_recv.at[n, way, hop - 1], up if way == 0 else down)
+    def w_slot(n, way, hop):
+        origin = lax.rem(z + 8 - hop, 8) if way == 0 else lax.rem(z + hop, 8)
+        return wbuf.at[n, origin]
+
+    def w_send_on(n, way, hop):
+        slot = w_slot(n, way, hop - 1)
+        copy = remote(slot, slot, w_send.at[n, way, hop - 1], w_recv.at[n, way, hop - 1], down if way else up)
+        copy.start()
+        sent.append(copy)
 
     def w_arrived(n, way, hop):
-        origin = lax.rem(z + 8 - hop, 8) if way == 0 else lax.rem(z + hop, 8)
-        slot = wbuf.at[n, origin]
-        remote(slot, slot, w_send.at[n, way, hop - 1], w_recv.at[n, way, hop - 1], up if way == 0 else down).wait_recv()
-
-    def w_start(n, hop):
+        slot = w_slot(n, way, hop)
+        remote(slot, slot, w_send.at[n, way, hop - 1], w_recv.at[n, way, hop - 1], down if way else up).wait_recv()
+
+    def start(n):
         for way in range(2):
-            if hop <= hops(n, way):
-                copy = w_copy(n, way, hop)
-                copy.start()
-                sent.append(copy)
-
-    def w_wait(n, hop):
-        for way in range(2):
-            if hop <= hops(n, way):
-                w_arrived(n, way, hop)
-
-    def w_pass(n, hop):
-        for way in range(2):
-            if hop <= hops(n, way):
-                w_arrived(n, way, hop)
-                if hop + 1 <= hops(n, way):
-                    copy = w_copy(n, way, hop + 1)
-                    copy.start()
-                    sent.append(copy)
-
-    for n in GROUPS[0]:
-        w_start(n, 1)
+            w_send_on(n, way, 1)
+
+    def relay(n, hop, way):
+        w_arrived(n, way, hop)
+        w_send_on(n, way, hop + 1)
+
+    for n in (0, 1, 2):
+        start(n)
 
     for k, (dx, dy) in enumerate(moves):
         xx, yy = plane(dx, dy)
@@ -184,11 +175,7 @@
     sine = jnp.sin(angles)
     rots[1] = jnp.where(lane < 64, -sine, sine)
 
-    for hop in range(1, 4):
-        for n in GROUPS[0]:
-            w_pass(n, hop)
-
-    for dx in range(4):
+    def hand_on(dx):
         for dy in range(4):
             if (dx, dy) == (0, 0):
                 continue
@@ -201,14 +188,17 @@
         copy = remote(block, block, f_send.at[dx], f_recv.at[dx], sibling)
         copy.start()
         sent.append(copy)
-    for n in GROUPS[1]:
-        w_start(n, 1)
-    for dx in range(4):
-        xx, _ = plane(-dx, 0)
-        block = abuf.at[lax.rem(xx, 2) * 2 + (1 - c), pl.ds((xx // 2) * 4, 4)]
-        remote(block, block, f_send.at[dx], f_recv.at[dx], sibling).wait_recv()
+
+    def rows_ready():
+        for dx in range(4):
+            xx, _ = plane(-dx, 0)
+            block = abuf.at[lax.rem(xx, 2) * 2 + (1 - c), pl.ds((xx // 2) * 4, 4)]
+            remote(block, block, f_send.at[dx], f_recv.at[dx], sibling).wait_recv()
 
     def product(n):
+        for way in range(2):
+            w_arrived(n, way, hops(n, way))
+
         def half(r):
             total = jnp.zeros((512, CHUNK), f32)
             for q in range(4):
@@ -245,31 +235,25 @@
         remote(ref, ref, p_send.at[n, slot], p_recv.at[n, slot], across).wait_recv()
         return rbuf[n, slot].astype(f32)
 
-    def second_step(n):
+    def second(n, dy):
         if X_FIRST[n]:
-            for dy in (2, 1, 3):
-                total = pbuf[n, xh * 4 + along(dy)].astype(f32) + arrived(n, dy)
-                qbuf[n, dy - 1] = total.astype(bf16)
-                copy = remote(
-                    qbuf.at[n, dy - 1], rbuf.at[n, 3 + dy], p_send.at[n, 3 + dy], p_recv.at[n, 3 + dy],
-                    at(z, x, along(dy), c),
-                )
-                copy.start()
-                sent.append(copy)
+            total = pbuf[n, xh * 4 + along(dy)].astype(f32) + arrived(n, dy)
+            slot, device = 3 + dy, at(z, x, along(dy), c)
         else:
             total = pbuf[n, far_place].astype(f32)
-            for dy in (1, 3, 2):
-                total += arrived(n, dy - 1)
-            qbuf[n, 0] = total.astype(bf16)
-            copy = remote(qbuf.at[n, 0], rbuf.at[n, 6], p_send.at[n, 6], p_recv.at[n, 6], across)
-            copy.start()
-            sent.append(copy)
+            for other in range(3):
+                total += arrived(n, other)
+            slot, device = 6, across
+        qbuf[n, slot - 4] = total.astype(bf16)
+        copy = remote(qbuf.at[n, slot - 4], rbuf.at[n, slot], p_send.at[n, slot], p_recv.at[n, slot], device)
+        copy.start()
+        sent.append(copy)
 
     def summed(n):
         total = pbuf[n, place].astype(f32)
         for slot in (0, 4, 6, 5) if X_FIRST[n] else (3, 5, 4, 6):
             total += arrived(n, slot)
-        return total * scale
+        return total * scales[0]
 
     def rotated(block):
         heads = []
@@ -278,21 +262,21 @@
             heads.append((head * rots[0] + pltpu.roll(head, 64, 1) * rots[1]).astype(bf16))
         return heads
 
-    for n in GROUPS[0]:
-        w_wait(n, 4)
-        product(n)
-
-    for k in range(1, 4):
-        slot = ssb.at[lax.rem(t + 4 - k, 4)]
-        remote(slot, slot, s_send.at[k - 1], s_recv.at[k - 1], sibling).wait_recv()
-    squares = ssb[0, 0:1, :] + ssb[1, 0:1, :] + ssb[2, 0:1, :] + ssb[3, 0:1, :]
-    scale = lax.rsqrt(to_column(squares) * (1.0 / WIDTH) + norm_eps)
-
-    slot = pdb.at[1 - side]
-    remote(slot, slot, d_send, d_recv, partner).wait_recv()
-    key_pos = jnp.concatenate([pdb[0, 0:1, :], pdb[1, 0:1, :]], axis=1)
-    key_doc = jnp.concatenate([pdb[0, 1:2, :], pdb[1, 1:2, :]], axis=1)
-    allowed = (key_pos <= pos_col) & (key_doc == doc_col)
+    def row_scale():
+        for k in range(1, 4):
+            slot = ssb.at[lax.rem(t + 4 - k, 4)]
+            remote(slot, slot, s_send.at[k - 1], s_recv.at[k - 1], sibling).wait_recv()
+        squares = ssb[0, 0:1, :] + ssb[1, 0:1, :] + ssb[2, 0:1, :] + ssb[3, 0:1, :]
+        scales.append(lax.rsqrt(to_column(squares) * (1.0 / WIDTH) + norm_eps))
+
+    def key_mask():
+        slot = pdb.at[1 - side]
+        remote(slot, slot, d_send, d_recv, partner).wait_recv()
+        key_pos = jnp.concatenate([pdb[0, 0:1, :], pdb[1, 0:1, :]], axis=1)
+        key_doc = jnp.concatenate([pdb[0, 1:2, :], pdb[1, 1:2, :]], axis=1)
+        masks.append((key_pos <= pos_col) & (key_doc == doc_col))
+
+    scales, masks = [], []
 
     def share(j):
         rows = kvb.at[j, side]
@@ -319,7 +303,7 @@
             score = lax.dot_general(
                 queries[h], key, (((1,), (1,)), ((), ())), preferred_element_type=f32
             ) * (HEAD ** -0.5)
-            score = jnp.where(allowed, score, -1e30)
+            score = jnp.where(masks[0], score, -1e30)
             top = jnp.max(score, axis=1, keepdims=True)
             expo = jnp.exp(score - top)
             norm = jnp.sum(expo, axis=1, keepdims=True)
@@ -332,28 +316,27 @@
             slot = kvb.at[j, 1 - side]
             remote(slot, slot, k_send.at[j], k_recv.at[j], partner).wait_recv()
 
-    for n in GROUPS[1]:
-        w_pass(n, 1)
-    for n in GROUPS[1]:
-        w_pass(n, 2)
-    second_step(0)
-    second_step(1)
-    for n in GROUPS[1]:
-        w_pass(n, 3)
-    values()
-    keys()
-    for n in GROUPS[1]:
-        w_wait(n, 4)
-        product(n)
-    second_step(2)
-    joined()
-    attend(2)
-    second_step(3)
-    second_step(4)
-    attend(3)
-    second_step(5)
-    attend(4)
-    attend(5)
+    def finish(n):
+        (keys, values, attend)[min(n, 2)](*([n] if n >= 2 else []))
+
+    steps = (
+        (relay, 0, 1, 1), (relay, 0, 1, 0), (relay, 1, 1, 0), (relay, 1, 1, 1), (relay, 2, 1, 1),
+        (relay, 2, 1, 0), (relay, 0, 2, 1), (relay, 0, 2, 0), (relay, 1, 2, 1), (relay, 1, 2, 0), (start, 3),
+        (relay, 2, 2, 1), (relay, 2, 2, 0), (hand_on, 2), (relay, 0, 3, 0), (hand_on, 1), (relay, 1, 3, 1),
+        (hand_on, 0), (hand_on, 3), (relay, 3, 1, 1), (relay, 3, 1, 0), (rows_ready,), (start, 4), (start, 5),
+        (relay, 2, 3, 0), (product, 1), (product, 0), (relay, 3, 2, 0), (relay, 3, 2, 1), (relay, 4, 1, 1),
+        (relay, 4, 1, 0), (relay, 5, 1, 1), (relay, 5, 1, 0), (second, 1, 2), (product, 2), (relay, 3, 3, 1),
+        (second, 1, 1), (second, 0, 0), (second, 1, 3), (relay, 4, 2, 1), (relay, 4, 2, 0), (relay, 5, 2, 1),
+        (relay, 5, 2, 0), (product, 3), (finish, 0), (relay, 4, 3, 0), (relay, 5, 3, 1), (second, 2, 0),
+        (second, 3, 2), (second, 3, 1), (product, 4), (product, 5), (second, 3, 3), (finish, 1),
+        (second, 5, 2), (second, 5, 1), (second, 4, 0), (second, 5, 3), (joined,), (finish, 2), (finish, 3),
+        (finish, 4), (finish, 5),
+    )
+    for step in steps:
+        step[0](*step[1:])
+        if step[0] is rows_ready:
+            row_scale()
+            key_mask()
     for copy in sent:
         copy.wait_send()
 

time: 75.7 us -> 62.9 us (0.83)
  Pallas kernels: 73.9 us -> 61.1 us
    pallas_call x1, Pallas kernels: 73.9 us -> 61.1 us  [body(): pl.pallas_call(kernel, out_shape=jax.ShapeDtypeStruct((KEPT, 1024), bf16)...]
where the time goes in v3:
time: 62.9 us; the launch traced here: 62.8 us
  Pallas kernels  61.1 us (97%)
  local copies, waits for them, and re-layouts  1.67 us (3%)
    pallas_call x1, Pallas kernels, body(): pl.pallas_call(kernel, out_shape=jax.ShapeDtypeStruct((KEPT, 1024), bf16)...  61.1 us
    unnamed x1, local copies, waits for them, and re-layouts  1.67 us

profile of v3, /device:TPU:8, one launch (start us, length us, event | category | flops | bytes accessed | tf_op | source)
XLA Modules:
  0.0 62.8 jit_solution(8543057291370978968)
XLA Ops:
  0.0 61.1 %shard_map.64 = bf16[128,1024]{1,0:T(8,128)(2,1)} custom-call(bf16[256,2048]{1,0:T(8,128)(2,1)} %hidden_in.1, s32[1,128]{1,0:T(1,128)} %kept_in.1, s32[1,256]{1,0:T(1,128)} %bitcast.3, f32[64,128]{1,0:T(8,128)} %bitcast.2, bf16[128,1024]{1,0:T(8,128)(2,1)} %wq.1, bf16[128,2,256]{2,1,0:T(2,128)(2,1)} %wkv_in.1), custom_call_target="tpu_custom_call" | custom-call | tf_op jit(solution)/shard_map/pallas_call | solution.py:348
  61.1 1.7 %copy.8 = bf16[128,1024]{1,0:T(8,128)(2,1)} copy(bf16[128,1024]{1,0:T(8,128)(2,1)} %shard_map.64) | data formatting | bytes 524288

commit v4 on v3

--- a/solution.py
+++ b/solution.py
@@ -19,7 +19,8 @@
 norm_eps = 1e-05
 rope_base = 10000.0
 
-X_FIRST = (False, True, False, True, False, True)
+BEHIND = 40
+X_FIRST = (True, False, True, True, False, True)
 
 
 def kernel(
@@ -49,19 +50,6 @@
     partner = (s + 1 - 2 * side, t)
     moves = [(dx, dy) for dx in range(4) for dy in range(4) if (dx, dy) != (0, 0)]
     moves.sort(key=lambda m: -min(m[0], 4 - m[0]) - min(m[1], 4 - m[1]))
-
-    barrier = pltpu.get_barrier_semaphore()
-
-    def greet(device):
-        pl.semaphore_signal(barrier, inc=1, device_id=device, device_id_type=MESH)
-
-    greet(up)
-    greet(down)
-    for dx, dy in moves:
-        xx, yy = plane(dx, dy)
-        greet(at(z, xx, yy, c))
-    greet(sibling)
-    greet((s, (1 - xl) * 2 + (1 - c)))
 
     loads = [
         pltpu.make_async_copy(src, dst, load_sem.at[i])
@@ -79,6 +67,61 @@
     for load in loads:
         load.start()
 
+    barrier = pltpu.get_barrier_semaphore()
+
+    def greet(device):
+        pl.semaphore_signal(barrier, inc=1, device_id=device, device_id_type=MESH)
+
+    greet(up)
+    greet(down)
+    for dx, dy in moves:
+        xx, yy = plane(dx, dy)
+        greet(at(z, xx, yy, c))
+    greet(sibling)
+    greet((s, (1 - xl) * 2 + (1 - c)))
+
+    for load in loads[4:]:
+        load.wait()
+    wbuf[0, z] = wkv[:, 0, :]
+    wbuf[1, z] = wkv[:, 1, :]
+
+    pl.semaphore_wait(barrier, 19)
+
+    def remote(src, dst, send, recv, device):
+        return pltpu.make_async_remote_copy(
+            src_ref=src, dst_ref=dst, send_sem=send, recv_sem=recv, device_id=device, device_id_type=MESH
+        )
+
+    sent = []
+
+    def hops(n, way):
+        return 4 if (n + way) % 2 == 0 else 3
+
+    def w_slot(n, way, hop):
+        origin = lax.rem(z + 8 - hop, 8) if way == 0 else lax.rem(z + hop, 8)
+        return wbuf.at[n, origin]
+
+    def w_send_on(n, way, hop):
+        slot = w_slot(n, way, hop - 1)
+        copy = remote(slot, slot, w_send.at[n, way, hop - 1], w_recv.at[n, way, hop - 1], down if way else up)
+        copy.start()
+        sent.append(copy)
+
+    def w_arrived(n, way, hop):
+        slot = w_slot(n, way, hop)
+        remote(slot, slot, w_send.at[n, way, hop - 1], w_recv.at[n, way, hop - 1], down if way else up).wait_recv()
+
+    def start(n):
+        for way in range(2):
+            w_send_on(n, way, 1)
+
+    def relay(n, hop, way):
+        w_arrived(n, way, hop)
+        w_send_on(n, way, hop + 1)
+
+    for n in (0, 1, 2):
+        start(n)
+
     lane = lax.broadcasted_iota(jnp.int32, (KEPT, KEPT), 1)
     eye = lax.broadcasted_iota(jnp.int32, (KEPT, KEPT), 0) == lane
 
@@ -114,47 +157,6 @@
             asrc[to, :, high * 128 : (high + 1) * 128] = scaled.astype(bf16)
     ssb[t, 0:1, :] = to_row(square)
     abuf[t, place] = asrc[place]
-    for load in loads[4:]:
-        load.wait()
-    wbuf[0, z] = wkv[:, 0, :]
-    wbuf[1, z] = wkv[:, 1, :]
-
-    pl.semaphore_wait(barrier, 19)
-
-    def remote(src, dst, send, recv, device):
-        return pltpu.make_async_remote_copy(
-            src_ref=src, dst_ref=dst, send_sem=send, recv_sem=recv, device_id=device, device_id_type=MESH
-        )
-
-    sent = []
-
-    def hops(n, way):
-        return 4 if (n + way) % 2 == 0 else 3
-
-    def w_slot(n, way, hop):
-        origin = lax.rem(z + 8 - hop, 8) if way == 0 else lax.rem(z + hop, 8)
-        return wbuf.at[n, origin]
-
-    def w_send_on(n, way, hop):
-        slot = w_slot(n, way, hop - 1)
-        copy = remote(slot, slot, w_send.at[n, way, hop - 1], w_recv.at[n, way, hop - 1], down if way else up)
-        copy.start()
-        sent.append(copy)
-
-    def w_arrived(n, way, hop):
-        slot = w_slot(n, way, hop)
-        remote(slot, slot, w_send.at[n, way, hop - 1], w_recv.at[n, way, hop - 1], down if way else up).wait_recv()
-
-    def start(n):
-        for way in range(2):
-            w_send_on(n, way, 1)
-
-    def relay(n, hop, way):
-        w_arrived(n, way, hop)
-        w_send_on(n, way, hop + 1)
-
-    for n in (0, 1, 2):
-        start(n)
 
     for k, (dx, dy) in enumerate(moves):
         xx, yy = plane(dx, dy)
@@ -320,24 +322,28 @@
         (keys, values, attend)[min(n, 2)](*([n] if n >= 2 else []))
 
     steps = (
-        (relay, 0, 1, 1), (relay, 0, 1, 0), (relay, 1, 1, 0), (relay, 1, 1, 1), (relay, 2, 1, 1),
-        (relay, 2, 1, 0), (relay, 0, 2, 1), (relay, 0, 2, 0), (relay, 1, 2, 1), (relay, 1, 2, 0), (start, 3),
-        (relay, 2, 2, 1), (relay, 2, 2, 0), (hand_on, 2), (relay, 0, 3, 0), (hand_on, 1), (relay, 1, 3, 1),
-        (hand_on, 0), (hand_on, 3), (relay, 3, 1, 1), (relay, 3, 1, 0), (rows_ready,), (start, 4), (start, 5),
-        (relay, 2, 3, 0), (product, 1), (product, 0), (relay, 3, 2, 0), (relay, 3, 2, 1), (relay, 4, 1, 1),
-        (relay, 4, 1, 0), (relay, 5, 1, 1), (relay, 5, 1, 0), (second, 1, 2), (product, 2), (relay, 3, 3, 1),
-        (second, 1, 1), (second, 0, 0), (second, 1, 3), (relay, 4, 2, 1), (relay, 4, 2, 0), (relay, 5, 2, 1),
-        (relay, 5, 2, 0), (product, 3), (finish, 0), (relay, 4, 3, 0), (relay, 5, 3, 1), (second, 2, 0),
-        (second, 3, 2), (second, 3, 1), (product, 4), (product, 5), (second, 3, 3), (finish, 1),
-        (second, 5, 2), (second, 5, 1), (second, 4, 0), (second, 5, 3), (joined,), (finish, 2), (finish, 3),
-        (finish, 4), (finish, 5),
+        (relay, 0, 1, 0), (relay, 0, 1, 1), (relay, 1, 1, 0), (relay, 1, 1, 1), (relay, 2, 1, 1),
+        (relay, 2, 1, 0), (relay, 0, 2, 0), (relay, 0, 2, 1), (relay, 1, 2, 1), (relay, 1, 2, 0),
+        (relay, 2, 2, 1), (relay, 2, 2, 0), (hand_on, 2), (relay, 0, 3, 0), (hand_on, 1), (start, 3),
+        (relay, 1, 3, 1), (start, 4), (start, 5), (hand_on, 3), (hand_on, 0), (relay, 2, 3, 0), (rows_ready,),
+        (product, 0), (relay, 3, 1, 1), (relay, 3, 1, 0), (product, 1), (relay, 4, 1, 1), (relay, 4, 1, 0),
+        (relay, 5, 1, 1), (relay, 5, 1, 0), (product, 2), (relay, 3, 2, 1), (relay, 3, 2, 0), (second, 0, 1),
+        (second, 0, 2), (relay, 4, 2, 0), (relay, 4, 2, 1), (second, 0, 3), (second, 1, 0), (relay, 5, 2, 0),
+        (relay, 5, 2, 1), (relay, 3, 3, 1), (second, 2, 2), (second, 2, 1), (relay, 4, 3, 0), (second, 2, 3),
+        (relay, 5, 3, 1), (finish, 0), (product, 3), (product, 4), (finish, 1), (product, 5), (second, 4, 0),
+        (second, 3, 3), (second, 3, 1), (second, 5, 2), (second, 3, 2), (joined,), (second, 5, 1),
+        (finish, 2), (second, 5, 3), (finish, 4), (finish, 3), (finish, 5),
     )
+    waited = 0
     for step in steps:
+        while len(sent) - waited > BEHIND:
+            sent[waited].wait_send()
+            waited += 1
         step[0](*step[1:])
         if step[0] is rows_ready:
             row_scale()
             key_mask()
-    for copy in sent:
+    for copy in sent[waited:]:
         copy.wait_send()
 
 

time: 62.9 us -> 62.4 us (level)
  no operation moved by 1% of the time
where the time goes in v4:
time: 62.4 us; the launch traced here: 62.3 us
  Pallas kernels  60.6 us (97%)
  local copies, waits for them, and re-layouts  1.67 us (3%)
    pallas_call x1, Pallas kernels, body(): pl.pallas_call(kernel, out_shape=jax.ShapeDtypeStruct((KEPT, 1024), bf16)...  60.6 us
    unnamed x1, local copies, waits for them, and re-layouts  1.67 us

profile of v4, /device:TPU:8, one launch (start us, length us, event | category | flops | bytes accessed | tf_op | source)
XLA Modules:
  0.0 62.3 jit_solution(8067045256912519619)
XLA Ops:
  0.0 60.6 %shard_map.64 = bf16[128,1024]{1,0:T(8,128)(2,1)} custom-call(bf16[256,2048]{1,0:T(8,128)(2,1)} %hidden_in.1, s32[1,128]{1,0:T(1,128)} %kept_in.1, s32[1,256]{1,0:T(1,128)} %bitcast.3, f32[64,128]{1,0:T(8,128)} %bitcast.2, bf16[128,1024]{1,0:T(8,128)(2,1)} %wq.1, bf16[128,2,256]{2,1,0:T(2,128)(2,1)} %wkv_in.1), custom_call_target="tpu_custom_call" | custom-call | tf_op jit(solution)/shard_map/pallas_call | solution.py:354
  60.6 1.7 %copy.8 = bf16[128,1024]{1,0:T(8,128)(2,1)} copy(bf16[128,1024]{1,0:T(8,128)(2,1)} %shard_map.64) | data formatting | bytes 524288

commit v5 on v4

--- a/solution.py
+++ b/solution.py
@@ -19,8 +19,8 @@
 norm_eps = 1e-05
 rope_base = 10000.0
 
-BEHIND = 40
-X_FIRST = (True, False, True, True, False, True)
+BEHIND = 24
+X_FIRST = (False, True, False, True, True, False)
 
 
 def kernel(
@@ -322,17 +322,17 @@
         (keys, values, attend)[min(n, 2)](*([n] if n >= 2 else []))
 
     steps = (
-        (relay, 0, 1, 0), (relay, 0, 1, 1), (relay, 1, 1, 0), (relay, 1, 1, 1), (relay, 2, 1, 1),
+        (relay, 0, 1, 0), (relay, 0, 1, 1), (relay, 1, 1, 1), (relay, 1, 1, 0), (relay, 2, 1, 1),
         (relay, 2, 1, 0), (relay, 0, 2, 0), (relay, 0, 2, 1), (relay, 1, 2, 1), (relay, 1, 2, 0),
-        (relay, 2, 2, 1), (relay, 2, 2, 0), (hand_on, 2), (relay, 0, 3, 0), (hand_on, 1), (start, 3),
-        (relay, 1, 3, 1), (start, 4), (start, 5), (hand_on, 3), (hand_on, 0), (relay, 2, 3, 0), (rows_ready,),
-        (product, 0), (relay, 3, 1, 1), (relay, 3, 1, 0), (product, 1), (relay, 4, 1, 1), (relay, 4, 1, 0),
-        (relay, 5, 1, 1), (relay, 5, 1, 0), (product, 2), (relay, 3, 2, 1), (relay, 3, 2, 0), (second, 0, 1),
-        (second, 0, 2), (relay, 4, 2, 0), (relay, 4, 2, 1), (second, 0, 3), (second, 1, 0), (relay, 5, 2, 0),
-        (relay, 5, 2, 1), (relay, 3, 3, 1), (second, 2, 2), (second, 2, 1), (relay, 4, 3, 0), (second, 2, 3),
-        (relay, 5, 3, 1), (finish, 0), (product, 3), (product, 4), (finish, 1), (product, 5), (second, 4, 0),
-        (second, 3, 3), (second, 3, 1), (second, 5, 2), (second, 3, 2), (joined,), (second, 5, 1),
-        (finish, 2), (second, 5, 3), (finish, 4), (finish, 3), (finish, 5),
+        (relay, 2, 2, 1), (relay, 2, 2, 0), (relay, 0, 3, 0), (start, 3), (hand_on, 2), (hand_on, 1),
+        (relay, 1, 3, 1), (start, 4), (hand_on, 3), (hand_on, 0), (start, 5), (rows_ready,), (product, 0),
+        (relay, 2, 3, 0), (relay, 3, 1, 1), (relay, 3, 1, 0), (product, 1), (relay, 4, 1, 1),
+        (relay, 4, 1, 0), (relay, 5, 1, 1), (relay, 5, 1, 0), (product, 2), (relay, 3, 2, 1),
+        (relay, 3, 2, 0), (second, 1, 2), (relay, 4, 2, 1), (relay, 4, 2, 0), (second, 0, 0),
+        (relay, 5, 2, 1), (relay, 5, 2, 0), (second, 1, 1), (second, 1, 3), (relay, 3, 3, 1), (second, 2, 0),
+        (relay, 4, 3, 0), (finish, 0), (relay, 5, 3, 1), (product, 3), (product, 4), (finish, 1),
+        (product, 5), (second, 3, 2), (joined,), (second, 3, 1), (second, 5, 0), (second, 3, 3), (finish, 2),
+        (second, 4, 2), (second, 4, 1), (second, 4, 3), (finish, 3), (finish, 5), (finish, 4),
     )
     waited = 0
     for step in steps:

time: 62.4 us -> 61.3 us (0.982)
  Pallas kernels: 60.6 us -> 59.5 us
    pallas_call x1, Pallas kernels: 60.6 us -> 59.5 us  [body(): pl.pallas_call(kernel, out_shape=jax.ShapeDtypeStruct((KEPT, 1024), bf16)...]
where the time goes in v5:
time: 61.3 us; the launch traced here: 61.2 us
  Pallas kernels  59.5 us (97%)
  local copies, waits for them, and re-layouts  1.67 us (3%)
    pallas_call x1, Pallas kernels, body(): pl.pallas_call(kernel, out_shape=jax.ShapeDtypeStruct((KEPT, 1024), bf16)...  59.5 us
    unnamed x1, local copies, waits for them, and re-layouts  1.67 us

profile of v5, /device:TPU:8, one launch (start us, length us, event | category | flops | bytes accessed | tf_op | source)
XLA Modules:
  0.0 61.2 jit_solution(3387380209571747372)
XLA Ops:
  0.0 59.5 %shard_map.64 = bf16[128,1024]{1,0:T(8,128)(2,1)} custom-call(bf16[256,2048]{1,0:T(8,128)(2,1)} %hidden_in.1, s32[1,128]{1,0:T(1,128)} %kept_in.1, s32[1,256]{1,0:T(1,128)} %bitcast.3, f32[64,128]{1,0:T(8,128)} %bitcast.2, bf16[128,1024]{1,0:T(8,128)(2,1)} %wq.1, bf16[128,2,256]{2,1,0:T(2,128)(2,1)} %wkv_in.1), custom_call_target="tpu_custom_call" | custom-call | tf_op jit(solution)/shard_map/pallas_call | solution.py:354
  59.5 1.7 %copy.8 = bf16[128,1024]{1,0:T(8,128)(2,1)} copy(bf16[128,1024]{1,0:T(8,128)(2,1)} %shard_map.64) | data formatting | bytes 524288

commit v6 on v5

--- a/solution.py
+++ b/solution.py
@@ -211,11 +211,14 @@
                 )
             pbuf[n, pl.ds(r * 4, 4)] = total.astype(bf16).reshape(4, KEPT, CHUNK)
 
-        pl.loop(0, 2)(half)
-        for slot, block, device in first_step(n):
-            copy = remote(pbuf.at[n, block], rbuf.at[n, slot], p_send.at[n, slot], p_recv.at[n, slot], device)
-            copy.start()
-            sent.append(copy)
+        steps_out = first_step(n)
+        far = 4 if X_FIRST[n] else 3
+        for r, group in ((1 - xh, steps_out[:far]), (xh, steps_out[far:])):
+            half(r)
+            for slot, block, device in group:
+                copy = remote(pbuf.at[n, block], rbuf.at[n, slot], p_send.at[n, slot], p_recv.at[n, slot], device)
+                copy.start()
+                sent.append(copy)
 
     across = at(z, lax.rem(x + 2, 4), y, c)
     far_place = (1 - xh) * 4 + y

time: 61.3 us -> 61.5 us (level)
  no operation moved by 1% of the time
where the time goes in v6:
time: 61.5 us; the launch traced here: 61.4 us
  Pallas kernels  59.7 us (97%)
  local copies, waits for them, and re-layouts  1.67 us (3%)
    pallas_call x1, Pallas kernels, body(): pl.pallas_call(kernel, out_shape=jax.ShapeDtypeStruct((KEPT, 1024), bf16)...  59.7 us
    unnamed x1, local copies, waits for them, and re-layouts  1.67 us

profile of v6, /device:TPU:8, one launch (start us, length us, event | category | flops | bytes accessed | tf_op | source)
XLA Modules:
  0.0 61.4 jit_solution(3169362447585154905)
XLA Ops:
  0.0 59.7 %shard_map.64 = bf16[128,1024]{1,0:T(8,128)(2,1)} custom-call(bf16[256,2048]{1,0:T(8,128)(2,1)} %hidden_in.1, s32[1,128]{1,0:T(1,128)} %kept_in.1, s32[1,256]{1,0:T(1,128)} %bitcast.3, f32[64,128]{1,0:T(8,128)} %bitcast.2, bf16[128,1024]{1,0:T(8,128)(2,1)} %wq.1, bf16[128,2,256]{2,1,0:T(2,128)(2,1)} %wkv_in.1), custom_call_target="tpu_custom_call" | custom-call | tf_op jit(solution)/shard_map/pallas_call | solution.py:357
  59.7 1.7 %copy.8 = bf16[128,1024]{1,0:T(8,128)(2,1)} copy(bf16[128,1024]{1,0:T(8,128)(2,1)} %shard_map.64) | data formatting | bytes 524288
